TPU v7x, 32 devices: a whole 2x2x4 slice. The times are simulated.
32 devices in a mesh: tm: 4 (over z), space: 4 (over x, core), node: 2 (over y).
Axes of the slice: x: 2, y: 2, z: 4, core: 2. Of those that a mesh axis runs over, the one named last changes fastest.
Arguments:
- initial: float32 [8, 64, 256], P(None, 'space'), may hold values from -6 to 6
- forcing: float32 [4, 8, 64, 256], P('tm', None, 'space'), may hold values from -6 to 6
- decay_rate: float32 [8, 64, 256], P(None, 'space'), may hold values from 0.02 to 20
- mixing: float32 [8, 8], replicated, may hold values from -2 to 2
- diffusivity: float32 [8], replicated, may hold values from 0.3 to 2
- velocity: float32 [3, 8], replicated, may hold values from -2 to 2
Outputs:
- node_values: float32 [4, 2, 8, 64, 256], P('tm', 'node', None, 'space')
All inputs are finite; a program needn't handle non-finite values.
Results may differ from a plain program's by a relative error of at most 0.0003.
Values sent between devices are 32-bit elements; how exact they have to be, the bound alone decides.
A program may use at most 64 MiB of HBM per device.

v0:
```python
import jax
import jax.numpy as jnp
import numpy as np
from jax import lax
from jax.sharding import PartitionSpec as P

NZ = 16


time_step = 0.05


def carried_in(part, axis, combine, identity):
    place = lax.axis_index(axis)
    gathered = jax.tree.map(lambda a: lax.all_gather(a, axis), part)
    state = jax.tree.map(lambda a, e: jnp.zeros_like(a) + jnp.asarray(e, a.dtype), part, identity)

    def one(lap, state):
        return combine(
            state, jax.tree.map(lambda a: lax.dynamic_index_in_dim(a, lap, 0, False), gathered)
        )

    return lax.fori_loop(0, place, one, state)


def extended(value, sides, width):
    for axis, dim in sides:
        peers, length = (lax.axis_size(axis), value.shape[dim])
        up = [(i, (i + 1) % peers) for i in range(peers - 1)]
        down = [(j, i) for i, j in up]
        last = lax.slice_in_dim(value, length - width, length, axis=dim)
        initial = lax.slice_in_dim(value, 0, width, axis=dim)
        before = lax.ppermute(last, axis, up)
        after = lax.ppermute(initial, axis, down)
        value = jnp.concatenate([before, value, after], axis=dim)
    return value


def from_behind(block, axis, distance):
    devices = range(lax.axis_size(axis))
    route = [(i - distance, i) for i in devices if i - distance in devices]
    return lax.ppermute(block, axis, route)


def quadrature(node_count):
    points = [(position + 1.0) / node_count for position in range(node_count)]
    weights_table = np.zeros((node_count, node_count))
    for column in range(node_count):
        coeffs = [1.0]
        denominator = 1.0
        for other_node in range(node_count):
            if other_node != column:
                shifted = [0.0] + coeffs
                for degree in range(len(coeffs)):
                    shifted[degree] = shifted[degree] - points[other_node] * coeffs[degree]
                coeffs = shifted
                denominator = denominator * (points[column] - points[other_node])
        for row_node in range(node_count):
            running = 0.0
            for degree in range(len(coeffs)):
                running = running + coeffs[degree] * points[row_node] ** (degree + 1) / (degree + 1)
            weights_table[row_node, column] = running / denominator
    return (weights_table, np.array(points))


def rate_of(padded, decay_rate, mixing, diffusivity, velocity, force_now):
    center = padded[:, 1:-1]
    x_plus = padded[:, 2:]
    x_minus = padded[:, :-2]
    y_plus = jnp.roll(center, -NZ, axis=2)
    y_minus = jnp.roll(center, NZ, axis=2)
    depth_index = jnp.arange(center.shape[2]) % NZ
    z_plus = jnp.where(depth_index == NZ - 1, 0.0, jnp.roll(center, -1, axis=2))
    z_minus = jnp.where(depth_index == 0, 0.0, jnp.roll(center, 1, axis=2))
    laplace = x_plus + x_minus + (y_plus + y_minus) + (z_plus + z_minus) - 6.0 * center
    drift_term = (
        velocity[0][:, None, None] * (x_plus - x_minus)
        + velocity[1][:, None, None] * (y_plus - y_minus)
        + velocity[2][:, None, None] * (z_plus - z_minus)
    )
    coupled = jnp.tanh(jnp.einsum("ts,sxc->txc", mixing, center, precision=lax.Precision.HIGHEST))
    return (
        diffusivity[:, None, None] * laplace
        - 0.5 * drift_term
        - decay_rate * center
        + coupled
        + force_now
    )


def body(initial, forcing, decay_rate, mixing, diffusivity, velocity):
    node_count = lax.axis_size("node")
    node_index = lax.axis_index("node")
    weights_table, points = quadrature(node_count)
    q_table = jnp.asarray(weights_table, jnp.float32)
    time_table = jnp.asarray(points, jnp.float32)
    own_match = jnp.arange(node_count) == node_index
    own_row = jnp.sum(jnp.where(own_match[:, None], q_table, 0.0), axis=0)
    last_row = q_table[node_count - 1]
    own_time = jnp.sum(jnp.where(own_match, time_table, 0.0))
    last_time = time_table[node_count - 1]
    stiff_part = time_step * (own_time / node_count) * decay_rate
    last_stiff = time_step * (last_time / node_count) * decay_rate
    force_now = forcing[0]
    factor = 1.0 / (1.0 + time_step * decay_rate)
    offset = time_step * force_now * factor

    def compose(earlier, later):
        return (earlier[0] * later[0], later[0] * earlier[1] + later[1])

    prefix = carried_in(
        (factor, offset), "tm", compose, (jnp.ones_like(factor), jnp.zeros_like(offset))
    )
    slice_start = prefix[0] * initial + prefix[1]

    def local_rate(field_now):
        padded = extended(field_now, (("space", 1),), 1)
        return rate_of(padded, decay_rate, mixing, diffusivity, velocity, force_now)

    def weighted_sums(field_now):
        rate_now = local_rate(field_now)
        empty = jnp.zeros_like(rate_now)
        shard_piece = lax.all_gather(rate_now[None], "node", axis=0, tiled=True)
        return (
            empty + jnp.sum(own_row[:, None, None, None] * shard_piece, axis=0),
            empty + jnp.sum(last_row[:, None, None, None] * shard_piece, axis=0),
        )

    first_value = (slice_start + own_time * time_step * force_now) / (
        1.0 + own_time * time_step * decay_rate
    )
    last_first = (slice_start + last_time * time_step * force_now) / (
        1.0 + last_time * time_step * decay_rate
    )
    own_sum, end_sum = weighted_sums(first_value)
    second_value = (slice_start + time_step * own_sum + stiff_part * first_value) / (
        1.0 + stiff_part
    )
    end_value = (slice_start + time_step * end_sum + last_stiff * last_first) / (1.0 + last_stiff)
    handed = from_behind(end_value, "tm", 1)
    second_start = jnp.where(lax.axis_index("tm") == 0, initial, handed)
    own_next, unused_end = weighted_sums(second_value)
    final_value = (second_start + time_step * own_next + stiff_part * second_value) / (
        1.0 + stiff_part
    )
    return final_value[None, None]


def solution(mesh):
    placed = (
        P(None, "space", None),
        P("tm", None, "space", None),
        P(None, "space", None),
        P(),
        P(),
        P(),
    )
    return jax.shard_map(
        body,
        mesh=mesh,
        in_specs=placed,
        out_specs=P("tm", "node", None, "space", None),
        check_vma=False,
    )
```

profile of v0, /device:TPU:0, one launch (start us, length us, event | category | flops | bytes accessed | tf_op | source)
XLA Modules:
  0.0 68.4 jit_solution(13447236375832373844)
XLA Ops:
  0.0 1.2 %fusion.14 = (f32[8,16,256]{2,0,1:T(8,128)S(1)}, f32[8,16,256]{2,0,1:T(8,128)S(1)}) fusion(f32[1,8,16,256]{3,2,1,0:T(8,128)} %param.11, f32[8,16,256]{2,1,0:T(8,128)} %param.12), kind=kLoop, calls=%fused_computation.43 | loop fusion | flops 163840 | bytes 524288 | tf_op jit(solution)/shard_map/mul | solution.py:106
  1.2 17.4 %all-gather = f32[32,16,256]{2,0,1:T(8,128)S(1)} all-gather(f32[8,16,256]{2,0,1:T(8,128)S(1)} %get-tuple-element.96), channel_id=2, replica_groups=mesh['tm'=4,'space'=4,'node'=2] {'tm'}, dimensions={0}, use_global_device_ids=true | all-gather | bytes 655360 | tf_op jit(solution)/shard_map/all_gather | solution.py:15
  18.5 16.3 %all-gather.1 = f32[32,16,256]{2,0,1:T(8,128)S(1)} all-gather(f32[8,16,256]{2,0,1:T(8,128)S(1)} %get-tuple-element.95), channel_id=3, replica_groups=mesh['tm'=4,'space'=4,'node'=2] {'tm'}, dimensions={0}, use_global_device_ids=true | all-gather | bytes 655360 | tf_op jit(solution)/shard_map/all_gather | solution.py:15
  34.9 0.7 %copy-done.8 = f32[2]{0:T(128)S(1)} copy-done((f32[2]{0:T(128)S(1)}, f32[2]{0:T(128)}, u32[]{:S(2)}) %copy-start.8) | copy-done | bytes 32
  35.6 0.6 select_reduce_fusion.1
  36.9 0.4 fusion.12
  37.3 1.3 %collective-permute-start = (f32[8,1,256]{2,0,1:T(8,128)S(1)}, f32[8,1,256]{2,0,1:T(8,128)S(1)}, u32[]{:S(2)}, u32[]{:S(2)}) collective-permute-start(f32[8,1,256]{2,0,1:T(8,128)S(1)} %get-tuple-element.86), channel_id=1, source_target_pairs={{2,0},{4,2},{6,4},{3,1},{5,3},{7,5},{10,8},{12,10},{14,12},{11,9},... | collective-permute-start | bytes 24584 | tf_op jit(solution)/shard_map/ppermute | solution.py:34
  38.6 3.0 %collective-permute-start.1 = (f32[8,1,256]{2,0,1:T(8,128)S(1)}, f32[8,1,256]{2,0,1:T(8,128)S(1)}, u32[]{:S(2)}, u32[]{:S(2)}) collective-permute-start(f32[8,1,256]{2,0,1:T(8,128)S(1)} %get-tuple-element.85), channel_id=1, source_target_pairs={{0,2},{2,4},{4,6},{1,3},{3,5},{5,7},{8,10},{10,12},{12,14},{9,11},... | collective-permute-start | bytes 24584 | tf_op jit(solution)/shard_map/ppermute | solution.py:33
  41.7 0.1 fusion.23
  41.8 0.1 fusion.25
  41.9 0.1 fusion.24
  42.0 0.1 fusion.26
  42.0 0.6 copy-done.4
  42.6 0.7 copy-done.5
  43.3 0.1 select_reduce_fusion
  44.1 0.6 copy-done.7
  44.7 0.4 fusion.6
  45.1 6.9 %all-gather.2 = f32[16,16,256]{2,0,1:T(8,128)S(1)} all-gather(f32[8,16,256]{2,0,1:T(8,128)S(1)} %fusion.6), channel_id=4, replica_groups=mesh['tm'=4,'space'=4,'node'=2] {'node'}, dimensions={0}, use_global_device_ids=true | all-gather | bytes 393216 | tf_op jit(solution)/shard_map/all_gather | solution.py:123
  52.0 0.1 fusion.9
  52.2 0.2 add_divide_fusion.1
  52.4 0.1 fusion.18
  52.5 0.1 fusion.20
  52.6 0.1 fusion.19
  52.7 1.3 %collective-permute-start.3 = (f32[8,1,256]{2,0,1:T(8,128)S(1)}, f32[8,1,256]{2,0,1:T(8,128)S(1)}, u32[]{:S(2)}, u32[]{:S(2)}) collective-permute-start(f32[8,1,256]{2,0,1:T(8,128)S(1)} %get-tuple-element.76), channel_id=1, source_target_pairs={{2,0},{4,2},{6,4},{3,1},{5,3},{7,5},{10,8},{12,10},{14,12},{11,9},... | collective-permute-start | bytes 24584 | tf_op jit(solution)/shard_map/ppermute | solution.py:34
  54.0 3.0 %collective-permute-start.4 = (f32[8,1,256]{2,0,1:T(8,128)S(1)}, f32[8,1,256]{2,0,1:T(8,128)S(1)}, u32[]{:S(2)}, u32[]{:S(2)}) collective-permute-start(f32[8,1,256]{2,0,1:T(8,128)S(1)} %get-tuple-element.75), channel_id=1, source_target_pairs={{0,2},{2,4},{4,6},{1,3},{3,5},{5,7},{8,10},{10,12},{12,14},{9,11},... | collective-permute-start | bytes 24584 | tf_op jit(solution)/shard_map/ppermute | solution.py:33
  57.0 0.1 fusion.21
  57.1 2.9 %collective-permute-start.2 = (f32[8,16,256]{2,0,1:T(8,128)S(1)}, f32[8,16,256]{2,0,1:T(8,128)S(1)}, u32[]{:S(2)}, u32[]{:S(2)}) collective-permute-start(f32[8,16,256]{2,0,1:T(8,128)S(1)} %get-tuple-element.73), channel_id=1, source_target_pairs={{0,8},{8,16},{16,24},{1,9},{9,17},{17,25},{2,10},{10,18},{18,26},{... | collective-permute-start | bytes 393224 | tf_op jit(solution)/shard_map/ppermute | solution.py:42
  60.1 0.4 fusion.7
  60.4 6.9 %all-gather.3 = f32[16,16,256]{2,0,1:T(8,128)S(1)} all-gather(f32[8,16,256]{2,0,1:T(8,128)S(1)} %fusion.7), channel_id=5, replica_groups=mesh['tm'=4,'space'=4,'node'=2] {'node'}, dimensions={0}, use_global_device_ids=true | all-gather | bytes 393216 | tf_op jit(solution)/shard_map/all_gather | solution.py:123
  67.4 0.1 fusion.8
  67.5 0.2 divide_bitcast_fusion
  67.7 0.7 %copy.40 = f32[1,1,8,16,256]{4,3,2,1,0:T(8,128)} copy(f32[1,1,8,16,256]{4,2,3,1,0:T(8,128)S(1)} %divide_bitcast_fusion) | data formatting | bytes 262144 | tf_op jit(solution)/shard_map/broadcast_in_dim | solution.py:146
  (27 shorter events, 0.1 us)
Async XLA Ops:
  0.0 44.1 %copy-start = (f32[8,8]{1,0:T(8,128)S(1)}, f32[8,8]{1,0:T(8,128)}, u32[]{:S(2)}) copy-start(f32[8,8]{1,0:T(8,128)} %param.13) | copy-start | bytes 772
  34.9 2.0 %copy-start.1 = (f32[8,16,256]{2,1,0:T(8,128)S(1)}, f32[8,16,256]{2,1,0:T(8,128)}, u32[]{:S(2)}) copy-start(f32[8,16,256]{2,1,0:T(8,128)} %param.12) | copy-start | bytes 393220
  34.9 2.0 %copy-start.2 = (f32[1,8,16,256]{3,2,1,0:T(8,128)S(1)}, f32[1,8,16,256]{3,2,1,0:T(8,128)}, u32[]{:S(2)}) copy-start(f32[1,8,16,256]{3,2,1,0:T(8,128)} %param.11) | copy-start | bytes 393220
  34.9 2.0 %copy-start.3 = (f32[8,16,256]{2,1,0:T(8,128)S(1)}, f32[8,16,256]{2,1,0:T(8,128)}, u32[]{:S(2)}) copy-start(f32[8,16,256]{2,1,0:T(8,128)} %param.10) | copy-start | bytes 393220
  34.9 0.7 %copy-start.8 = (f32[2]{0:T(128)S(1)}, f32[2]{0:T(128)}, u32[]{:S(2)}) copy-start(f32[2]{0:T(128)} %constant.68.clone) | copy-start | bytes 28
  37.3 6.7 %collective-permute-start = (f32[8,1,256]{2,0,1:T(8,128)S(1)}, f32[8,1,256]{2,0,1:T(8,128)S(1)}, u32[]{:S(2)}, u32[]{:S(2)}) collective-permute-start(f32[8,1,256]{2,0,1:T(8,128)S(1)} %get-tuple-element.86), channel_id=1, source_target_pairs={{2,0},{4,2},{6,4},{3,1},{5,3},{7,5},{10,8},{12,10},{14,12},{11,9},... | collective-permute-start | bytes 24584 | tf_op jit(solution)/shard_map/ppermute | solution.py:34
  38.6 5.5 %collective-permute-start.1 = (f32[8,1,256]{2,0,1:T(8,128)S(1)}, f32[8,1,256]{2,0,1:T(8,128)S(1)}, u32[]{:S(2)}, u32[]{:S(2)}) collective-permute-start(f32[8,1,256]{2,0,1:T(8,128)S(1)} %get-tuple-element.85), channel_id=1, source_target_pairs={{0,2},{2,4},{4,6},{1,3},{3,5},{5,7},{8,10},{10,12},{12,14},{9,11},... | collective-permute-start | bytes 24584 | tf_op jit(solution)/shard_map/ppermute | solution.py:33
  41.9 0.7 %copy-start.4 = (f32[3,8]{1,0:T(4,128)S(1)}, f32[3,8]{1,0:T(4,128)}, u32[]{:S(2)}) copy-start(f32[3,8]{1,0:T(4,128)} %param.15) | copy-start | bytes 292
  42.6 0.7 copy-start.5
  44.1 0.7 copy-start.7
  45.1 6.9 %copy-start.6 = (f32[2]{0:T(128)S(1)}, f32[2]{0:T(128)}, u32[]{:S(2)}) copy-start(f32[2]{0:T(128)} %constant.71) | copy-start | bytes 28
  52.7 7.4 %collective-permute-start.3 = (f32[8,1,256]{2,0,1:T(8,128)S(1)}, f32[8,1,256]{2,0,1:T(8,128)S(1)}, u32[]{:S(2)}, u32[]{:S(2)}) collective-permute-start(f32[8,1,256]{2,0,1:T(8,128)S(1)} %get-tuple-element.76), channel_id=1, source_target_pairs={{2,0},{4,2},{6,4},{3,1},{5,3},{7,5},{10,8},{12,10},{14,12},{11,9},... | collective-permute-start | bytes 24584 | tf_op jit(solution)/shard_map/ppermute | solution.py:34
  54.0 6.1 %collective-permute-start.4 = (f32[8,1,256]{2,0,1:T(8,128)S(1)}, f32[8,1,256]{2,0,1:T(8,128)S(1)}, u32[]{:S(2)}, u32[]{:S(2)}) collective-permute-start(f32[8,1,256]{2,0,1:T(8,128)S(1)} %get-tuple-element.75), channel_id=1, source_target_pairs={{0,2},{2,4},{4,6},{1,3},{3,5},{5,7},{8,10},{10,12},{12,14},{9,11},... | collective-permute-start | bytes 24584 | tf_op jit(solution)/shard_map/ppermute | solution.py:33
  57.1 10.4 %collective-permute-start.2 = (f32[8,16,256]{2,0,1:T(8,128)S(1)}, f32[8,16,256]{2,0,1:T(8,128)S(1)}, u32[]{:S(2)}, u32[]{:S(2)}) collective-permute-start(f32[8,16,256]{2,0,1:T(8,128)S(1)} %get-tuple-element.73), channel_id=1, source_target_pairs={{0,8},{8,16},{16,24},{1,9},{9,17},{17,25},{2,10},{10,18},{18,26},{... | collective-permute-start | bytes 393224 | tf_op jit(solution)/shard_map/ppermute | solution.py:42
where the time goes:
time: 68.7 us; the launch traced here: 68.4 us
  blocking collectives  47.5 us (69%)
  starting transfers between devices  11.6 us (17%)
  local copies, waits for them, and re-layouts  4.09 us (6%)
  other arithmetic  2.83 us (4%)
  between operations  1.59 us (2%)
  matrix products  0.75 us (1%)
    all_gather x2, blocking collectives, carried_in(): gathered = jax.tree.map(lambda a: lax.all_gather(a, axis), part)  33.7 us
    all_gather x2, blocking collectives, weighted_sums(): shard_piece = lax.all_gather(rate_now[None], 'node', axis=0, tiled=True)  13.9 us
    ppermute x2, starting transfers between devices, extended(): before = lax.ppermute(last, axis, up)  6.06 us
    ppermute x1, starting transfers between devices, from_behind(): return lax.ppermute(block, axis, route)  2.94 us
    unnamed x18, local copies, waits for them, and re-layouts  2.66 us
    ppermute x2, starting transfers between devices, extended(): after = lax.ppermute(initial, axis, down)  2.58 us
  transfers between devices with their start and end apart: 5, of which 0 were waited for; matrix products, arithmetic and copies ran while one was open for 1% of the time, Pallas kernels for 0%

commit v1 on v0

v1 whole, which is shorter than its diff:
```python
import functools

import jax
import jax.numpy as jnp
import numpy as np
from jax import lax
from jax.experimental import pallas as pl
from jax.experimental.pallas import tpu as pltpu
from jax.sharding import PartitionSpec as P

NZ = 16
WIDTH = 2
TILE = 8

time_step = 0.05


def quadrature(node_count):
    points = [(position + 1.0) / node_count for position in range(node_count)]
    weights_table = np.zeros((node_count, node_count))
    for column in range(node_count):
        coeffs = [1.0]
        denominator = 1.0
        for other_node in range(node_count):
            if other_node != column:
                shifted = [0.0] + coeffs
                for degree in range(len(coeffs)):
                    shifted[degree] = shifted[degree] - points[other_node] * coeffs[degree]
                coeffs = shifted
                denominator = denominator * (points[column] - points[other_node])
        for row_node in range(node_count):
            running = 0.0
            for degree in range(len(coeffs)):
                running = running + coeffs[degree] * points[row_node] ** (degree + 1) / (degree + 1)
            weights_table[row_node, column] = running / denominator
    return (weights_table, np.array(points))


def kernel(
    slices, pieces, nodes,
    initial_hbm, forcing_hbm, decay_hbm, mix, diff, vel, out_hbm,
    start, force, decay, handed, following, grow, shift,
    node_inv, node_add, sweep_inv, own_inv,
    field, mixed, base, last_value, result,
    side_send, side_recv, edge_send, edge_first, edge_recv,
    load_sem, out_sem,
    side_ss, side_rs, edge_ss, first_ss, edge_rs, start_ss, start_rs, hand_ss, hand_rs,
):
    species, rows, cells = following.shape
    tiles = rows // TILE
    halo = slice(rows, rows + TILE)
    h = time_step
    table, points = quadrature(nodes)
    n = lax.axis_index("tm")
    p = lax.axis_index("space")
    m = lax.axis_index("node")
    has_left, has_right = p > 0, p < pieces - 1
    has_before, has_after = n > 0, n < slices - 1
    sides = ((has_left, p - 1), (has_right, p + 1))
    mesh_id = pl.DeviceIdType.MESH

    barrier = pltpu.get_barrier_semaphore()

    def greet(condition, where):
        @pl.when(condition)
        def _():
            pl.semaphore_signal(barrier, inc=1, device_id=where, device_id_type=mesh_id)

    greet(has_before, {"tm": n - 1})
    for present, place in sides:
        greet(present, {"space": place})
        greet(present & has_before, {"tm": n - 1, "space": place})

    load_force = pltpu.make_async_copy(forcing_hbm.at[0], force.at[:, 0:rows], load_sem.at[0])
    load_decay = pltpu.make_async_copy(decay_hbm, decay.at[:, 0:rows], load_sem.at[1])
    load_start = pltpu.make_async_copy(initial_hbm, start.at[:, 0:rows], load_sem.at[2])
    load_handed = pltpu.make_async_copy(initial_hbm, handed, load_sem.at[3])
    load_force.start()
    load_decay.start()

    @pl.when(n == 0)
    def _():
        load_start.start()
        load_handed.start()

    zero_tile = jnp.zeros((species, TILE, cells), jnp.float32)
    start[:, halo, :] = zero_tile
    force[:, halo, :] = zero_tile
    decay[:, halo, :] = zero_tile

    def send(src, dst, ss, rs, where):
        return pltpu.make_async_remote_copy(
            src_ref=src, dst_ref=dst, send_sem=ss, recv_sem=rs, device_id=where, device_id_type=mesh_id
        )

    def side_copy(k):
        return send(side_send.at[k], side_recv.at[1 - k], side_ss.at[k], side_rs.at[1 - k], {"space": sides[k][1]})

    def first_copy(k):
        return send(edge_first.at[k], edge_recv.at[1 - k], first_ss.at[k], edge_rs.at[1 - k], {"space": sides[k][1]})

    def edge_copy(k):
        return send(
            edge_send.at[k], edge_recv.at[1 - k], edge_ss.at[k], edge_rs.at[1 - k],
            {"tm": n + 1, "space": sides[k][1]},
        )

    def start_copy(s):
        return send(following.at[s], start.at[s, 0:rows], start_ss.at[s], start_rs.at[s], {"tm": n + 1})

    def hand_copy(t):
        part = pl.ds(TILE * t, TILE)
        return send(last_value.at[:, part], handed.at[:, part], hand_ss.at[t], hand_rs.at[t], {"tm": n + 1})

    def pack(dst, offset, src, s):
        low = offset + WIDTH * s
        dst[0, low:low + WIDTH, :] = src[s, 0:WIDTH, :]
        dst[1, low:low + WIDTH, :] = src[s, rows - WIDTH:rows, :]

    def unpack(dst, src, k, offset):
        for s in range(species):
            low = offset + WIDTH * s
            if k == 0:
                dst[s, rows + TILE - WIDTH:rows + TILE, :] = src[0, low:low + WIDTH, :]
            else:
                dst[s, rows:rows + WIDTH, :] = src[1, low:low + WIDTH, :]

    load_force.wait()
    load_decay.wait()
    whole = slice(0, rows)
    for s in range(species):
        inverse = 1.0 / (1.0 + h * decay[s, whole, :])
        grow[s] = inverse
        shift[s] = h * force[s, whole, :] * inverse
        pack(side_send, 0, force, s)
        pack(side_send, WIDTH * species, decay, s)

    def present_count(flag):
        return flag.astype(jnp.int32)

    beside = present_count(has_left) + present_count(has_right)
    pl.semaphore_wait(barrier, beside + present_count(has_after) * (1 + beside))

    def pass_on(s):
        following[s] = grow[s] * start[s, whole, :] + shift[s]

        @pl.when(has_after)
        def _():
            start_copy(s).start()

        pack(edge_send, 0, following, s)

    def pass_edges():
        for k in range(2):
            @pl.when(has_after & sides[k][0])
            def _():
                edge_copy(k).start()

    @pl.when(n == 0)
    def _():
        load_start.wait()
        for s in range(species):
            pass_on(s)
        pass_edges()
        for s in range(species):
            pack(edge_first, 0, start, s)
        for k in range(2):
            @pl.when(sides[k][0])
            def _():
                first_copy(k).start()

    for k in range(2):
        @pl.when(sides[k][0])
        def _():
            side_copy(k).start()

    own_time = jnp.float32(0.0)
    own_row = [jnp.float32(0.0)] * nodes
    for i in range(nodes):
        own_time = jnp.where(m == i, jnp.float32(points[i]), own_time)
        own_row = [jnp.where(m == i, jnp.float32(table[i, j]), own_row[j]) for j in range(nodes)]
    own_stiff = own_time * jnp.float32(h / nodes)

    def prepare(s, part):
        d = decay[s, part, :]
        f = force[s, part, :]
        for j in range(nodes):
            inverse = 1.0 / (1.0 + float(points[j] * h) * d)
            node_inv[j, s, part, :] = inverse
            node_add[j, s, part, :] = float(points[j] * h) * f * inverse
            sweep_inv[j, s, part, :] = 1.0 / (1.0 + float(h * points[j] / nodes) * d)

    for s in range(species):
        prepare(s, whole)
        own_inv[s] = 1.0 / (1.0 + own_stiff * decay[s, whole, :])
    for k in range(2):
        @pl.when(sides[k][0])
        def _():
            side_copy(1 - k).wait_recv()
            unpack(force, side_recv, k, 0)
            unpack(decay, side_recv, k, WIDTH * species)
    for s in range(species):
        prepare(s, halo)

    def node_values(s, part):
        w = start[s, part, :]
        return [w * node_inv[j, s, part, :] + node_add[j, s, part, :] for j in range(nodes)]

    def interior_values(s):
        values = node_values(s, whole)
        for j in range(nodes):
            field[j, s, TILE:TILE + rows, :] = values[j]
            field[j, s, 2 * TILE + rows:3 * TILE + rows, :] = values[j][0:TILE]

    @pl.when(n == 0)
    def _():
        for s in range(species):
            interior_values(s)

    @pl.when(has_before)
    def _():
        for s in range(species):
            start_copy(s).wait_recv()
            pass_on(s)
            interior_values(s)
        pass_edges()

    for k in range(2):
        @pl.when(sides[k][0])
        def _():
            edge_copy(1 - k).wait_recv()
            unpack(start, edge_recv, k, 0)
    for s in range(species):
        values = node_values(s, halo)
        for j in range(nodes):
            field[j, s, 0:TILE, :] = values[j]
            field[j, s, TILE + rows:2 * TILE + rows, :] = values[j]

    depth = lax.broadcasted_iota(jnp.int32, (TILE, cells), 1) % NZ
    is_first, is_last = depth == 0, depth == NZ - 1
    row = lax.broadcasted_iota(jnp.int32, (TILE, cells), 0)
    inside = ((row < WIDTH) & has_right) | ((row >= TILE - WIDTH) & has_left)

    def linear(ref, s, low, d):
        c = ref[s, low:low + TILE, :]
        x_plus = ref[s, low + 1:low + TILE + 1, :]
        x_minus = ref[s, low - 1:low + TILE - 1, :]
        y_plus = pltpu.roll(c, cells - NZ, 1)
        y_minus = pltpu.roll(c, NZ, 1)
        z_plus = jnp.where(is_last, 0.0, pltpu.roll(c, cells - 1, 1))
        z_minus = jnp.where(is_first, 0.0, pltpu.roll(c, 1, 1))
        dd = diff[s]
        vx, vy, vz = 0.5 * vel[0, s], 0.5 * vel[1, s], 0.5 * vel[2, s]
        return (
            ((dd - vx) * x_plus + (dd + vx) * x_minus)
            + ((dd - vy) * y_plus + (dd + vy) * y_minus)
            + ((dd - vz) * z_plus + (dd + vz) * z_minus)
            - (6.0 * dd + d) * c
        )

    def coupled(values, s):
        total = mix[s, 0] * values[0]
        for t in range(1, species):
            total = total + mix[s, t] * values[t]
        return jnp.tanh(total)

    for t in list(range(tiles)) + [tiles]:
        part = slice(TILE * t, TILE * t + TILE)
        low = TILE * (t + 1)
        is_halo = t == tiles
        fresh = [[None] * species for _ in range(nodes)]
        centers = [[field[j, s, low:low + TILE, :] for s in range(species)] for j in range(nodes)]
        for s in range(species):
            d = decay[s, part, :]
            f = force[s, part, :]
            w = start[s, part, :]
            rates = [linear(field.at[j], s, low, d) + coupled(centers[j], s) + f for j in range(nodes)]
            for i in range(nodes):
                total = float(h * table[i, 0]) * rates[0]
                for j in range(1, nodes):
                    total = total + float(h * table[i, j]) * rates[j]
                v = (w + total + float(h * points[i] / nodes) * d * centers[i][s]) * sweep_inv[i, s, part, :]
                fresh[i][s] = jnp.where(inside, v, 0.0) if is_halo else v
            if not is_halo:
                last_value[s, part, :] = fresh[nodes - 1][s]
            sum_now = own_row[0] * fresh[0][s]
            for j in range(1, nodes):
                sum_now = sum_now + own_row[j] * fresh[j][s]
            mixed[s, low:low + TILE, :] = sum_now
            if is_halo:
                mixed[s, 0:TILE, :] = sum_now
        if not is_halo:
            @pl.when(has_after)
            def _():
                hand_copy(t).start()

            for s in range(species):
                gained = own_time * force[s, part, :]
                own = fresh[0][s]
                for j in range(nodes):
                    gained = gained + own_row[j] * coupled(fresh[j], s)
                    if j > 0:
                        own = jnp.where(m == j, fresh[j][s], own)
                base[s, part, :] = h * gained + own_stiff * decay[s, part, :] * own

    for t in range(tiles):
        part = slice(TILE * t, TILE * t + TILE)
        for s in range(species):
            rate = linear(mixed, s, TILE * (t + 1), decay[s, part, :])
            base[s, part, :] = (base[s, part, :] + h * rate) * own_inv[s, part, :]

    @pl.when(n == 0)
    def _():
        load_handed.wait()

    def out_copy(t):
        part = pl.ds(TILE * t, TILE)
        return pltpu.make_async_copy(result.at[:, part], out_hbm.at[0, 0, :, part], out_sem.at[t])

    for t in range(tiles):
        part = slice(TILE * t, TILE * t + TILE)

        @pl.when(has_before)
        def _():
            hand_copy(t).wait_recv()

        result[:, part, :] = handed[:, part, :] * own_inv[:, part, :] + base[:, part, :]
        out_copy(t).start()

    for k in range(2):
        @pl.when(sides[k][0])
        def _():
            side_copy(k).wait_send()

        @pl.when(sides[k][0] & (n == 0))
        def _():
            first_copy(k).wait_send()

        @pl.when(sides[k][0] & has_after)
        def _():
            edge_copy(k).wait_send()

    @pl.when(has_after)
    def _():
        for s in range(species):
            start_copy(s).wait_send()
        for t in range(tiles):
            hand_copy(t).wait_send()

    for t in range(tiles):
        out_copy(t).wait()


def body(initial, forcing, decay_rate, mixing, diffusivity, velocity):
    slices, pieces, nodes = (lax.axis_size(a) for a in ("tm", "space", "node"))
    species, rows, cells = initial.shape
    longer = rows + TILE
    packed = WIDTH * species
    tiles = rows // TILE
    f32 = jnp.float32
    dma = pltpu.SemaphoreType.DMA
    hbm = pl.BlockSpec(memory_space=pl.ANY)
    smem = pl.BlockSpec(memory_space=pltpu.SMEM)
    plain = pltpu.VMEM((species, rows, cells), f32)
    extended = pltpu.VMEM((species, longer, cells), f32)
    per_node = pltpu.VMEM((nodes, species, longer, cells), f32)
    return pl.pallas_call(
        functools.partial(kernel, slices, pieces, nodes),
        out_shape=jax.ShapeDtypeStruct((1, 1, species, rows, cells), f32),
        in_specs=[hbm, hbm, hbm, smem, smem, smem],
        out_specs=hbm,
        scratch_shapes=[
            extended, extended, extended, plain, plain, plain, plain,
            per_node, per_node, per_node, plain,
            pltpu.VMEM((nodes, species, rows + 3 * TILE, cells), f32),
            pltpu.VMEM((species, rows + 2 * TILE, cells), f32),
            plain, plain, plain,
            pltpu.VMEM((2, 2 * packed, cells), f32),
            pltpu.VMEM((2, 2 * packed, cells), f32),
            pltpu.VMEM((2, packed, cells), f32),
            pltpu.VMEM((2, packed, cells), f32),
            pltpu.VMEM((2, packed, cells), f32),
            dma((4,)), dma((tiles,)),
            dma((2,)), dma((2,)), dma((2,)), dma((2,)), dma((2,)),
            dma((species,)), dma((species,)), dma((tiles,)), dma((tiles,)),
        ],
        compiler_params=pltpu.CompilerParams(
            collective_id=0, has_side_effects=True, vmem_limit_bytes=60 * 1024 * 1024
        ),
    )(initial, forcing, decay_rate, mixing, diffusivity, velocity)


def solution(mesh):
    placed = (
        P(None, "space", None),
        P("tm", None, "space", None),
        P(None, "space", None),
        P(),
        P(),
        P(),
    )
    return jax.shard_map(
        body,
        mesh=mesh,
        in_specs=placed,
        out_specs=P("tm", "node", None, "space", None),
        check_vma=False,
    )
```

time: 68.7 us -> 17.6 us (0.26)
  the two profiles are of different devices: /device:TPU:0 before, /device:TPU:25 now
where the time goes in v1:
time: 17.6 us; the launch traced here: 17.4 us
  Pallas kernels  15.9 us (90%)
  local copies, waits for them, and re-layouts  1.57 us (9%)
    pallas_call x1, Pallas kernels, body(): pl.pallas_call(functools.partial(kernel, slices, pieces, nodes), out_shap...  15.9 us
    unnamed x1, local copies, waits for them, and re-layouts  1.57 us

profile of v1, /device:TPU:25, one launch (start us, length us, event | category | flops | bytes accessed | tf_op | source)
XLA Modules:
  0.0 17.4 jit_solution(12983065897990422525)
XLA Ops:
  0.0 15.9 %shard_map.64 = f32[1,1,8,16,256]{4,3,2,1,0:T(8,128)} custom-call(f32[8,16,256]{2,1,0:T(8,128)} %initial_hbm.1, f32[1,8,16,256]{3,2,1,0:T(8,128)} %forcing_hbm.1, f32[8,16,256]{2,1,0:T(8,128)} %decay_hbm.1, f32[8,8]{1,0:T(8,128)} %mix.1, f32[8]{0:T(128)} %diff.1, f32[3,8]{1,0:T(4,128)} %vel.1), custom_call_target="tpu_custom_call" | custom-call | tf_op jit(solution)/shard_map/pallas_call | solution.py:367
  15.9 1.6 %copy.8 = f32[1,1,8,16,256]{4,3,2,1,0:T(8,128)} copy(f32[1,1,8,16,256]{4,3,2,1,0:T(8,128)} %shard_map.64) | data formatting | bytes 262144

commit v2 on v1

--- a/solution.py
+++ b/solution.py
@@ -38,12 +38,12 @@
 
 def kernel(
     slices, pieces, nodes,
-    initial_hbm, forcing_hbm, decay_hbm, mix, diff, vel, out_hbm,
-    start, force, decay, handed, following, grow, shift,
+    initial_hbm, forcing_hbm, decay_hbm, mix_hbm, diff_hbm, vel_hbm, out_ref,
+    mix, diff, vel, start, force, decay, handed, following, grow, shift,
     node_inv, node_add, sweep_inv, own_inv,
-    field, mixed, base, last_value, result,
+    field, mixed, base, last_value,
     side_send, side_recv, edge_send, edge_first, edge_recv,
-    load_sem, out_sem,
+    load_sem,
     side_ss, side_rs, edge_ss, first_ss, edge_rs, start_ss, start_rs, hand_ss, hand_rs,
 ):
     species, rows, cells = following.shape
@@ -75,8 +75,14 @@
     load_decay = pltpu.make_async_copy(decay_hbm, decay.at[:, 0:rows], load_sem.at[1])
     load_start = pltpu.make_async_copy(initial_hbm, start.at[:, 0:rows], load_sem.at[2])
     load_handed = pltpu.make_async_copy(initial_hbm, handed, load_sem.at[3])
+    loads = [
+        pltpu.make_async_copy(src, dst, load_sem.at[4 + i])
+        for i, (src, dst) in enumerate([(mix_hbm, mix), (diff_hbm, diff), (vel_hbm, vel)])
+    ]
     load_force.start()
     load_decay.start()
+    for load in loads:
+        load.start()
 
     @pl.when(n == 0)
     def _():
@@ -236,6 +242,8 @@
             field[j, s, 0:TILE, :] = values[j]
             field[j, s, TILE + rows:2 * TILE + rows, :] = values[j]
 
+    for load in loads:
+        load.wait()
     depth = lax.broadcasted_iota(jnp.int32, (TILE, cells), 1) % NZ
     is_first, is_last = depth == 0, depth == NZ - 1
     row = lax.broadcasted_iota(jnp.int32, (TILE, cells), 0)
@@ -313,10 +321,6 @@
     def _():
         load_handed.wait()
 
-    def out_copy(t):
-        part = pl.ds(TILE * t, TILE)
-        return pltpu.make_async_copy(result.at[:, part], out_hbm.at[0, 0, :, part], out_sem.at[t])
-
     for t in range(tiles):
         part = slice(TILE * t, TILE * t + TILE)
 
@@ -324,8 +328,7 @@
         def _():
             hand_copy(t).wait_recv()
 
-        result[:, part, :] = handed[:, part, :] * own_inv[:, part, :] + base[:, part, :]
-        out_copy(t).start()
+        out_ref[0, 0, :, part, :] = handed[:, part, :] * own_inv[:, part, :] + base[:, part, :]
 
     for k in range(2):
         @pl.when(sides[k][0])
@@ -347,11 +350,9 @@
         for t in range(tiles):
             hand_copy(t).wait_send()
 
-    for t in range(tiles):
-        out_copy(t).wait()
-
-
-def body(initial, forcing, decay_rate, mixing, diffusivity, velocity):
+
+def body(*given):
+    initial, _, _, mixing, diffusivity, velocity = given
     slices, pieces, nodes = (lax.axis_size(a) for a in ("tm", "space", "node"))
     species, rows, cells = initial.shape
     longer = rows + TILE
@@ -359,35 +360,35 @@
     tiles = rows // TILE
     f32 = jnp.float32
     dma = pltpu.SemaphoreType.DMA
-    hbm = pl.BlockSpec(memory_space=pl.ANY)
-    smem = pl.BlockSpec(memory_space=pltpu.SMEM)
+    hbm = pl.BlockSpec(memory_space=pltpu.HBM)
     plain = pltpu.VMEM((species, rows, cells), f32)
     extended = pltpu.VMEM((species, longer, cells), f32)
     per_node = pltpu.VMEM((nodes, species, longer, cells), f32)
     return pl.pallas_call(
         functools.partial(kernel, slices, pieces, nodes),
         out_shape=jax.ShapeDtypeStruct((1, 1, species, rows, cells), f32),
-        in_specs=[hbm, hbm, hbm, smem, smem, smem],
-        out_specs=hbm,
+        in_specs=[hbm] * 6,
+        out_specs=pl.BlockSpec(memory_space=pltpu.VMEM),
         scratch_shapes=[
+            pltpu.SMEM(mixing.shape, f32), pltpu.SMEM(diffusivity.shape, f32), pltpu.SMEM(velocity.shape, f32),
             extended, extended, extended, plain, plain, plain, plain,
             per_node, per_node, per_node, plain,
             pltpu.VMEM((nodes, species, rows + 3 * TILE, cells), f32),
             pltpu.VMEM((species, rows + 2 * TILE, cells), f32),
-            plain, plain, plain,
+            plain, plain,
             pltpu.VMEM((2, 2 * packed, cells), f32),
             pltpu.VMEM((2, 2 * packed, cells), f32),
             pltpu.VMEM((2, packed, cells), f32),
             pltpu.VMEM((2, packed, cells), f32),
             pltpu.VMEM((2, packed, cells), f32),
-            dma((4,)), dma((tiles,)),
+            dma((7,)),
             dma((2,)), dma((2,)), dma((2,)), dma((2,)), dma((2,)),
             dma((species,)), dma((species,)), dma((tiles,)), dma((tiles,)),
         ],
         compiler_params=pltpu.CompilerParams(
-            collective_id=0, has_side_effects=True, vmem_limit_bytes=60 * 1024 * 1024
+            collective_id=0, has_side_effects=True, vmem_limit_bytes=24 * 1024 * 1024
         ),
-    )(initial, forcing, decay_rate, mixing, diffusivity, velocity)
+    )(*(pltpu.with_memory_space_constraint(a, pltpu.HBM) for a in given))
 
 
 def solution(mesh):

time: 17.6 us -> 15.3 us (0.87)
  Pallas kernels: 15.9 us -> 14.5 us
  local copies, waits for them, and re-layouts: 1.57 us -> 0.66 us
    pallas_call x1, Pallas kernels: 15.9 us -> 14.5 us  [body(): pl.pallas_call(functools.partial(kernel, slices, pieces, nodes), out_shap...]
    unnamed x1, local copies, waits for them, and re-layouts: 1.57 us -> 0.66 us
where the time goes in v2:
time: 15.3 us; the launch traced here: 15.1 us
  Pallas kernels  14.5 us (95%)
  local copies, waits for them, and re-layouts  0.66 us (4%)
    pallas_call x1, Pallas kernels, body(): pl.pallas_call(functools.partial(kernel, slices, pieces, nodes), out_shap...  14.5 us
    unnamed x1, local copies, waits for them, and re-layouts  0.66 us

profile of v2, /device:TPU:25, one launch (start us, length us, event | category | flops | bytes accessed | tf_op | source)
XLA Modules:
  0.0 15.1 jit_solution(13420729570752824874)
XLA Ops:
  0.0 14.5 %shard_map.64 = f32[1,1,8,16,256]{4,3,2,1,0:T(8,128)S(1)} custom-call(f32[8,16,256]{2,1,0:T(8,128)} %initial_hbm.1, f32[1,8,16,256]{3,2,1,0:T(8,128)} %forcing_hbm.1, f32[8,16,256]{2,1,0:T(8,128)} %decay_hbm.1, f32[8,8]{1,0:T(8,128)} %mix_hbm.1, f32[8]{0:T(128)} %diff_hbm.1, f32[3,8]{1,0:T(4,128)} %vel_hbm.1), custom_call_target="tpu_custom_call" | custom-call | tf_op jit(solution)/shard_map/pallas_call | solution.py:367
  14.5 0.7 %copy.8 = f32[1,1,8,16,256]{4,3,2,1,0:T(8,128)} copy(f32[1,1,8,16,256]{4,3,2,1,0:T(8,128)S(1)} %shard_map.64) | data formatting | bytes 262144
